TPU v7x, 32 devices: a whole 2x2x4 slice. The times are simulated.
32 devices in a mesh: section: 4 (over y, core), seq: 2 (over x), batch: 4 (over z).
Axes of the slice: x: 2, y: 2, z: 4, core: 2. Of those that a mesh axis runs over, the one named last changes fastest.
Arguments:
- latent: bfloat16 [4, 256, 3072], P('batch', 'seq'), may hold values from -6 to 6
- carried: bfloat16 [4, 256, 3072], P('batch', 'seq'), may hold values from -6 to 6
- samples: bfloat16 [4, 256, 3072], P('batch', 'seq'), may hold values from -6 to 6
- noise: bfloat16 [4, 256, 3072], P('batch', 'seq'), may hold values from -6 to 6
- gen_level: int32 [4], P('batch'), may hold values from 0 to 63
- score_level: int32 [4], P('batch'), may hold values from 0 to 63
- mod_table: float32 [4, 64, 3, 3072], P('section'), may hold values from -3 to 3
- qkv_weight: bfloat16 [4, 3072, 9216], P('section', ('seq', 'batch')), may hold values from -0.109375 to 0.109375
- out_weight: bfloat16 [4, 3072, 3072], P('section', None, ('seq', 'batch')), may hold values from -0.109375 to 0.109375
- query_gain: float32 [4, 128], P('section'), may hold values from 0.5 to 6
- key_gain: float32 [4, 128], P('section'), may hold values from 0.5 to 6
Outputs:
- block_out: bfloat16 [4, 4, 256, 3072], P('section', 'batch', 'seq')
- gen_grad: bfloat16 [4, 256, 3072], P('batch', 'seq', 'section')
All inputs are finite; a program needn't handle non-finite values. Where the computation divides by a largest or mean magnitude, that divisor is 1e-20 or more.
Results may differ from a plain program's by a relative error of at most 0.023.
The roundings to bfloat16 on the way count: a program that leaves them out, or rounds other values in their place, can miss the bound.
Values may be sent and summed in bfloat16 or wider, within the bound.
A program may use at most 128 MiB of HBM per device.

v0:
```python
import math

import jax
import jax.numpy as jnp
from jax import lax
from jax.sharding import PartitionSpec as P

HEADS = 24
HD = 128
LEVELS = 64


norm_eps = 1e-06
mean_eps = 1e-05


def from_root(value, axis, source):
    kept = jnp.where(lax.axis_index(axis) == source, value, 0).astype(value.dtype)
    return lax.psum(kept, axis)


def modulate(source, table, level):
    levels = table.shape[0]
    onehot = (jnp.arange(levels, dtype=jnp.int32) == level).astype(jnp.float32)
    picked = jnp.dot(onehot[None, :], table.reshape(levels, -1), precision=lax.Precision.HIGHEST)
    picked = picked.reshape(3, -1)
    data = source.astype(jnp.float32)
    center = data - jnp.mean(data, axis=-1, keepdims=True)
    spread = jnp.mean(center * center, axis=-1, keepdims=True)
    normed = center * lax.rsqrt(spread + norm_eps)
    return ((normed * (1.0 + picked[1]) + picked[0]).astype(jnp.bfloat16), picked[2])


def head_norm(raw, gain):
    power = jnp.mean(raw * raw, axis=-1, keepdims=True)
    return (raw * lax.rsqrt(power + norm_eps) * gain).astype(jnp.bfloat16)


def pair_attention(stacked):
    width = stacked.shape[-1]
    length = stacked.shape[2]
    scale = 1.0 / math.sqrt(width)
    step = 512 if length > 512 and length % 512 == 0 else length

    def one_pair(args):
        q_head, k_head, v_head = args
        query_blocks = q_head.reshape(length // step, step, width)

        def one_block(query_block):
            score = jnp.dot(query_block, k_head.T, preferred_element_type=jnp.float32) * scale
            top = jnp.max(score, axis=-1, keepdims=True)
            weight = jnp.exp(score - top)
            total = jnp.sum(weight, axis=-1, keepdims=True)
            mixed = jnp.dot(weight.astype(jnp.bfloat16), v_head, preferred_element_type=jnp.float32)
            return (mixed / total).astype(jnp.bfloat16)

        return lax.map(one_block, query_blocks).reshape(length, width)

    return lax.map(one_pair, (stacked[0], stacked[1], stacked[2]))


def head_attention(query, keys, values):
    count, rows, heads, width = query.shape
    stacked = jnp.stack([query, keys, values])
    stacked = jnp.transpose(stacked, (0, 1, 3, 2, 4)).reshape(3, count * heads, rows, width)
    regrouped = lax.all_to_all(stacked, "seq", split_axis=1, concat_axis=2, tiled=True)
    mixed = pair_attention(regrouped)
    back = lax.all_to_all(mixed, "seq", split_axis=1, concat_axis=0, tiled=True)
    back = back.reshape(count, heads, rows, width)
    return jnp.transpose(back, (0, 2, 1, 3))


def scaled_gap(samples, real, fake):
    gap = samples.astype(jnp.float32) - real.astype(jnp.float32)
    cells = lax.axis_size("seq") * gap.shape[0] * gap.shape[1]
    total = lax.psum(jnp.sum(jnp.abs(gap)), "seq")
    spread = total / cells + mean_eps
    return ((fake.astype(jnp.float32) - real.astype(jnp.float32)) / spread).astype(jnp.bfloat16)


def on_device(
    latent,
    carried,
    samples,
    noise,
    gen_level,
    score_level,
    mod_table,
    qkv_weight,
    out_weight,
    query_gain,
    key_gain,
):
    section = lax.axis_index("section")
    sigma = (score_level[0].astype(jnp.float32) + 1.0) / LEVELS
    noised = (
        (1.0 - sigma) * samples[0].astype(jnp.float32) + sigma * noise[0].astype(jnp.float32)
    ).astype(jnp.bfloat16)
    source = jnp.where(section == 0, latent[0], jnp.where(section == 1, carried[0], noised))
    level = jnp.where(section >= 2, score_level[0], gen_level[0])
    modulated, gate = modulate(source, mod_table[0], level)
    tok_rows = source.shape[0]
    qkv_local = qkv_weight[0]
    out_local = out_weight[0]
    q_gain = query_gain[0]
    k_gain = key_gain[0]
    groups = lax.axis_size("batch")
    local_rows = qkv_local.shape[0]
    own_heads = HEADS // groups
    mine = lax.all_to_all(
        qkv_local.reshape(local_rows, 3, HEADS, HD),
        "batch",
        split_axis=2,
        concat_axis=0,
        tiled=True,
    )
    mine = mine.reshape(local_rows * groups, 3 * own_heads * HD)
    everyone = lax.all_gather(modulated, "batch", axis=0, tiled=True)
    qkv = jnp.dot(
        everyone,
        lax.all_gather(mine, "seq", axis=0, tiled=True),
        preferred_element_type=jnp.float32,
    )
    qkv = qkv.reshape(groups, tok_rows, 3, own_heads, HD)
    query = head_norm(qkv[:, :, 0], q_gain)
    keys = head_norm(qkv[:, :, 1], k_gain)
    values = qkv[:, :, 2].astype(jnp.bfloat16)
    attended = head_attention(query, keys, values)
    attended = attended.reshape(groups * tok_rows, own_heads * HD)
    out_rows = lax.all_to_all(out_local, "batch", split_axis=0, concat_axis=1, tiled=True)
    out_rows = lax.all_gather(out_rows, "seq", axis=1, tiled=True)
    proj = lax.psum_scatter(
        jnp.dot(attended, out_rows, preferred_element_type=jnp.float32),
        "batch",
        scatter_dimension=0,
        tiled=True,
    )
    result = (source.astype(jnp.float32) + gate * proj).astype(jnp.bfloat16)
    real = from_root(result, "section", 2)
    fake = from_root(result, "section", 3)
    gen_grad = scaled_gap(samples[0], real, fake)
    col_width = gen_grad.shape[1] // lax.axis_size("section")
    own_cols = lax.dynamic_slice_in_dim(gen_grad, section * col_width, col_width, 1)
    return (result[None, None], own_cols[None])


def solution(mesh):
    return jax.shard_map(
        on_device,
        mesh=mesh,
        in_specs=(
            P("batch", "seq", None),
            P("batch", "seq", None),
            P("batch", "seq", None),
            P("batch", "seq", None),
            P("batch"),
            P("batch"),
            P("section", None, None, None),
            P("section", ("seq", "batch"), None),
            P("section", None, ("seq", "batch")),
            P("section", None),
            P("section", None),
        ),
        out_specs=(P("section", "batch", "seq", None), P("batch", "seq", "section")),
        check_vma=False,
    )
```

profile of v0, /device:TPU:0, one launch (start us, length us, event | category | flops | bytes accessed | tf_op | source)
XLA Modules:
  0.0 735.7 jit_solution(16406290928601330980)
XLA Ops:
  7.2 10.3 %copy.33 = bf16[1,384,9216]{1,2,0:T(8,128)(2,1)} copy(bf16[1,384,9216]{2,1,0:T(8,128)(2,1)} %param.20) | data formatting | bytes 14155776 | tf_op args[7]
  17.5 7.3 copy.34
  24.7 6.4 all-to-all-start
  32.5 1.6 copy.32
  34.1 1.3 copy.53
  35.5 2.5 convert_reduce_fusion
  39.3 1.3 fusion.20
  40.8 196.7 %all-to-all-done = bf16[384,3,24,128]{0,3,1,2:T(8,128)(2,1)} async-done(((bf16[384,3,24,128]{0,3,1,2:T(8,128)(2,1)}), bf16[384,3,24,128]{0,3,1,2:T(8,128)(2,1)}, u32[]{:S(2)}, u32[]{:S(2)}) %all-to-all-start) | async-done | bytes 7077920 | tf_op jit(solution)/shard_map/all_to_all | solution.py:110
  237.5 12.1 %copy.36 = bf16[4,384,3,6,128]{1,0,4,3,2:T(4,128)(2,1)} copy(bf16[4,384,3,6,128]{1,4,2,3,0:T(8,128)(2,1)} %bitcast.15) | data formatting | bytes 14155776 | tf_op jit(solution)/shard_map/all_to_all | solution.py:110
  249.5 7.1 copy.54
  256.6 3.9 all-to-all-start.3
  260.5 165.1 %all-gather.6.cloned.1.call-done = bf16[3072,2304]{0,1:T(8,128)(2,1)} async-done(((bf16[1536,2304]{0,1:T(8,128)(2,1)}), bf16[3072,2304]{0,1:T(8,128)(2,1)}) %all-gather.6.cloned.1.call-update) | async-done | bytes 14155792 | tf_op jit(solution)/shard_map/all_gather | solution.py:121
  425.7 13.1 %fusion.49 = f32[512,2304]{0,1:T(8,128)} fusion(bf16[512,3072]{1,0:T(8,128)(2,1)} %all-gather.4.cloned.1.call-done, bf16[3072,2304]{0,1:T(8,128)(2,1)} %all-gather.6.cloned.1.call-done), kind=kOutput, calls=%fused_computation.68 | convolution fusion | flops 7247757312 | bytes 22020096 | tf_op jit(solution)/shard_map/dot_general | solution.py:119
  438.8 6.3 reshape.132
  445.1 2.7 multiply_reduce_fusion.1
  447.8 1.7 fusion.30
  450.4 3.0 maximum_bitcast_fusion
  453.5 5.4 copy.51
  458.9 4.9 all-to-all-start.1
  463.9 2.7 copy.48
  466.6 38.0 %all-to-all-done.1 = bf16[3,24,128,128]{3,2,0,1:T(8,128)(2,1)} async-done(((bf16[3,24,128,128]{3,2,0,1:T(8,128)(2,1)}), bf16[3,24,128,128]{3,2,0,1:T(8,128)(2,1)}, u32[]{:S(2)}, u32[]{:S(2)}) %all-to-all-start.1) | async-done | bytes 2359328 | tf_op jit(solution)/shard_map/all_to_all | solution.py:66
  504.6 1.8 copy.40
  508.1 16.9 %while.10 = (s32[]{:T(128)}, bf16[12,256,128]{2,1,0:T(8,128)(2,1)S(1)}, bf16[12,256,128]{2,1,0:T(8,128)(2,1)S(1)}, bf16[12,256,128]{2,1,0:T(8,128)(2,1)S(1)}, bf16[12,256,128]{2,1,0:T(8,128)(2,1)}, /*index=5*/s32[]{:T(128)}) while((s32[]{:T(128)}, bf16[12,256,128]{2,1,0:T(8,128)(2,1)S(1)}, bf16[12,256,128]{2,1,0:T(8,128)(2,1)S(1)}, ...), condition=%wide.region_7.8_spmd, body=%wide.region_4.7_spmd.sunk | while | flops 34012672 | bytes 1055813 | solution.py:59
  508.4 1.1 fusion.63
  525.6 27.2 %all_to_all.64 = bf16[12,256,128]{2,0,1:T(8,128)(2,1)S(1)} all-to-all(bf16[12,256,128]{2,0,1:T(8,128)(2,1)S(1)} %copy.44), channel_id=1, replica_groups=mesh['section'=4,'seq'=2,'batch'=4] {'seq'}, dimensions={1} | all-to-all | bytes 1572864 | tf_op jit(solution)/shard_map/all_to_all | solution.py:68
  553.7 6.9 fusion.33
  560.8 110.8 %reduce-scatter.2.cloned.1.call-done = f32[128,3072]{1,0:T(8,128)} async-done(((f32[512,3072]{1,0:T(8,128)}), f32[128,3072]{1,0:T(8,128)}) %reduce-scatter.2.cloned.1.call-update) | async-done | bytes 1572880 | tf_op jit(solution)/shard_map/reduce_scatter | solution.py:132
  671.6 2.6 broadcast_select_fusion.1
  675.3 43.6 %all-reduce.3.cloned.1.call-done = (bf16[128,3072]{1,0:T(8,128)(2,1)}, bf16[128,3072]{1,0:T(8,128)(2,1)}) async-done(((bf16[128,3072]{1,0:T(8,128)(2,1)}, bf16[128,3072]{1,0:T(8,128)(2,1)}), (bf16[128,3072]{1,0:T(8,128)(2,1)}, bf16[128,3072]{1,0:T(8,128)(2,1)})) %all-reduce.3.cloned.1.call-update) | async-done | bytes 1572880 | tf_op jit(solution)/shard_map/psum | solution.py:19
  718.9 2.2 fusion.24
  721.3 5.6 psum.23
  727.5 1.7 fusion.38
  (81 shorter events, 22.6 us)
Async XLA Ops:
  24.7 7.8 %copy-start.4 = (f32[1,64,3,3072]{3,1,2,0:T(8,128)S(1)}, f32[1,64,3,3072]{3,1,2,0:T(8,128)}, u32[]{:S(2)}) copy-start(f32[1,64,3,3072]{3,1,2,0:T(8,128)} %param.19) | copy-start | bytes 7077892
  24.7 212.8 %all-to-all-start = ((bf16[384,3,24,128]{0,3,1,2:T(8,128)(2,1)}), bf16[384,3,24,128]{0,3,1,2:T(8,128)(2,1)}, u32[]{:S(2)}, u32[]{:S(2)}) async-start(bf16[384,3,24,128]{0,3,1,2:T(8,128)(2,1)} %copy.34), calls=%async_computation | async-start | bytes 14155776 | tf_op jit(solution)/shard_map/all_to_all | solution.py:110
  31.2 229.3 %all-gather.4.cloned.1.call-start = ((), (), s32[]{:S(2)}) async-start(), calls=%async_computation.5 | async-start | bytes 3932160 | tf_op jit(solution)/shard_map/all_gather | solution.py:118
  40.6 385.1 %all-gather.6.cloned.1.call-start = ((), (), s32[]{:S(2)}) async-start(), calls=%async_computation.6 | async-start | bytes 21233664 | tf_op jit(solution)/shard_map/all_gather | solution.py:121
  256.6 202.3 %all-to-all-start.3 = ((bf16[4,768,384]{2,1,0:T(8,128)(2,1)}), bf16[4,768,384]{2,1,0:T(8,128)(2,1)S(1)}, u32[]{:S(2)}, u32[]{:S(2)}) async-start(bf16[4,768,384]{2,1,0:T(8,128)(2,1)} %bitcast.127), calls=%async_computation.3 | async-start | bytes 4718592 | tf_op jit(solution)/shard_map/all_to_all | solution.py:130
  445.1 4.4 copy-start
  447.7 1.7 copy-start.6
  447.8 1.7 copy-start.7
  458.9 45.7 %all-to-all-start.1 = ((bf16[3,24,128,128]{3,2,0,1:T(8,128)(2,1)}), bf16[3,24,128,128]{3,2,0,1:T(8,128)(2,1)}, u32[]{:S(2)}, u32[]{:S(2)}) async-start(bf16[3,24,128,128]{3,2,0,1:T(8,128)(2,1)} %bitcast.121), calls=%async_computation.1 | async-start | bytes 4718592 | tf_op jit(solution)/shard_map/all_to_all | solution.py:66
  463.8 89.9 %all-gather.8.cloned.1.call-start = ((), (), s32[]{:S(2)}) async-start(), calls=%async_computation.7 | async-start | bytes 7077888 | tf_op jit(solution)/shard_map/all_gather | solution.py:131
  466.5 205.0 %reduce-scatter.2.cloned.1.call-start = ((), (), s32[]{:S(2)}) async-start(), calls=%async_computation.8 | async-start | bytes 7864320 | tf_op jit(solution)/shard_map/reduce_scatter | solution.py:132
  506.8 1.4 copy-start.5
  560.7 158.2 %all-reduce.3.cloned.1.call-start = ((), (), s32[]{:S(2)}) async-start(), calls=%async_computation.9 | async-start | bytes 3145728 | tf_op jit(solution)/shard_map/psum | solution.py:19
  674.2 1.1 copy-start.1
  674.2 44.7 %copy-start.3 = (bf16[1,128,3072]{2,1,0:T(8,128)(2,1)S(1)}, bf16[1,128,3072]{2,1,0:T(8,128)(2,1)}, u32[]{:S(2)}) copy-start(bf16[1,128,3072]{2,1,0:T(8,128)(2,1)} %param.15) | copy-start | bytes 2359300
  718.9 2.2 copy-start.2
Sparse Core Ops, SparseCore 0:
  40.7 111.8 all-gather.3
  256.7 168.8 all-gather.5
  466.7 87.0 all-gather.7
  560.8 110.7 reduce-scatter.1
  675.3 43.5 all-reduce.2
where the time goes:
time: 738 us; the launch traced here: 736 us
  waiting for transfers between devices  554 us (75%)
  local copies, waits for them, and re-layouts  60.7 us (8%)
  matrix products  36.7 us (5%)
  blocking collectives  32.8 us (4%)
  other arithmetic  19.3 us (3%)
  between operations  16 us (2%)
  starting transfers between devices  15.6 us (2%)
    all_to_all x1, waiting for transfers between devices, on_device(): lax.all_to_all(qkv_local.reshape(local_rows, 3, HEADS, HD), 'batch', spli...  197 us
    all_gather x1, waiting for transfers between devices, on_device(): lax.all_gather(mine, 'seq', axis=0, tiled=True)  165 us
    reduce_scatter x1, waiting for transfers between devices, on_device(): lax.psum_scatter(jnp.dot(attended, out_rows, preferred_element_type=jnp.f...  111 us
    psum x1, waiting for transfers between devices, from_root(): return lax.psum(kept, axis)  43.6 us
    all_to_all x1, waiting for transfers between devices, head_attention(): lax.all_to_all(stacked, 'seq', split_axis=1, concat_axis=2, tiled=True)  38 us
    all_to_all x1, blocking collectives, head_attention(): back = lax.all_to_all(mixed, 'seq', split_axis=1, concat_axis=0, tiled=True)  27.2 us
    unnamed x20, local copies, waits for them, and re-layouts  20.9 us
  transfers between devices with their start and end apart: 8, of which 6 were waited for; matrix products, arithmetic and copies ran while one was open for 11% of the time, Pallas kernels for 0%

commit v1 on v0

--- a/solution.py
+++ b/solution.py
@@ -1,8 +1,11 @@
+import functools
 import math
 
 import jax
 import jax.numpy as jnp
 from jax import lax
+from jax.experimental import pallas as pl
+from jax.experimental.pallas import tpu as pltpu
 from jax.sharding import PartitionSpec as P
 
 HEADS = 24
@@ -78,7 +81,7 @@
     return ((fake.astype(jnp.float32) - real.astype(jnp.float32)) / spread).astype(jnp.bfloat16)
 
 
-def on_device(
+def by_batch(
     latent,
     carried,
     samples,
@@ -144,7 +147,345 @@
     return (result[None, None], own_cols[None])
 
 
+MESH = pl.DeviceIdType.MESH
+
+
+def greet(peers):
+    barrier = pltpu.get_barrier_semaphore()
+    for peer in peers:
+        pl.semaphore_signal(barrier, inc=1, device_id=peer, device_id_type=MESH)
+    pl.semaphore_wait(barrier, len(peers))
+
+
+def group_peers(seqs, batches):
+    section, seq, batch = (lax.axis_index(name) for name in ("section", "seq", "batch"))
+    found = []
+    for near in range(batches):
+        for side in range(seqs):
+            to_seq = lax.rem(seq + side, seqs)
+            to_batch = lax.rem(batch + near, batches)
+            back_seq = lax.rem(seq - side + seqs, seqs)
+            back_batch = lax.rem(batch - near + batches, batches)
+            found.append(((section, to_seq, to_batch), (to_seq, to_batch), (back_seq, back_batch)))
+    return found
+
+
+def attend_kernel(
+    seqs, batches, w_ref, mod_ref, qg_ref, kg_ref, out_ref, wbuf, mbuf, acc, own_sem, w_send, w_recv, m_send, m_recv
+):
+    seq, batch = lax.axis_index("seq"), lax.axis_index("batch")
+    groups = seqs * batches
+    me = seq * batches + batch
+    depth = w_ref.shape[0]
+    width = w_ref.shape[1] // 3
+    share = width // groups
+    rows = mod_ref.shape[0]
+    length = rows * seqs
+    peers = group_peers(seqs, batches)
+    greet([coords for coords, _, _ in peers[1:]])
+
+    def columns(rank, part):
+        return pl.ds(pl.multiple_of(part * width + rank * share, 128), share)
+
+    my_rows = pl.ds(pl.multiple_of((batch * seqs + seq) * rows, rows), rows)
+    copies = []
+    for at, (coords, _, _) in enumerate(peers):
+        if at == 0:
+            continue
+        copy = pltpu.make_async_remote_copy(
+            mod_ref, mbuf.at[my_rows, :], m_send.at[at], m_recv.at[at], device_id=coords, device_id_type=MESH
+        )
+        copy.start()
+        copies.append(copy)
+    weights = []
+    for at, (coords, (to_seq, to_batch), _) in enumerate(peers):
+        rank = to_seq * batches + to_batch
+        for part in range(3):
+            source = w_ref.at[:, columns(rank, part)]
+            target = wbuf.at[me, :, pl.ds(part * share, share)]
+            if at == 0:
+                copy = pltpu.make_async_copy(source, target, own_sem.at[part])
+            else:
+                copy = pltpu.make_async_remote_copy(
+                    source,
+                    target,
+                    w_send.at[at, part],
+                    w_recv.at[at, part],
+                    device_id=coords,
+                    device_id_type=MESH,
+                )
+            copy.start()
+            weights.append(copy)
+    mbuf[my_rows, :] = mod_ref[...]
+    for copy in copies:
+        copy.wait()
+    for at, (_, _, (from_seq, from_batch)) in enumerate(peers):
+        for part in range(3):
+            weights[3 * at + part].wait()
+        rank = from_seq * batches + from_batch
+        deep = pl.ds(pl.multiple_of(rank * depth, 128), depth)
+
+        @pl.loop(0, batches)
+        def _(sample):
+            these = pl.ds(pl.multiple_of(sample * length, length), length)
+            term = jnp.dot(mbuf[these, deep], wbuf[rank], preferred_element_type=jnp.float32)
+            if at == 0:
+                acc[these, :] = term
+            else:
+                acc[these, :] += term
+
+    scale = 1.0 / math.sqrt(HD)
+
+    @pl.loop(0, batches)
+    def _(sample):
+        these = pl.ds(pl.multiple_of(sample * length, length), length)
+        for head in range(share // HD):
+            at = head * HD
+            query = head_norm(acc[these, at : at + HD], qg_ref[...])
+            keys = head_norm(acc[these, share + at : share + at + HD], kg_ref[...])
+            values = acc[these, 2 * share + at : 2 * share + at + HD].astype(jnp.bfloat16)
+            score = (
+                lax.dot_general(query, keys, (((1,), (1,)), ((), ())), preferred_element_type=jnp.float32) * scale
+            )
+            top = jnp.max(score, axis=-1, keepdims=True)
+            weight = jnp.exp(score - top)
+            total = jnp.sum(weight, axis=-1, keepdims=True)
+            mixed = jnp.dot(weight.astype(jnp.bfloat16), values, preferred_element_type=jnp.float32)
+            out_ref[these, at : at + HD] = (mixed / total).astype(jnp.bfloat16)
+
+
+def attend(seqs, batches, qkv_local, modulated, q_gain, k_gain):
+    groups = seqs * batches
+    depth, width = qkv_local.shape[0], qkv_local.shape[1] // 3
+    share = width // groups
+    rows = modulated.shape[0] * groups
+    return pl.pallas_call(
+        functools.partial(attend_kernel, seqs, batches),
+        out_shape=jax.ShapeDtypeStruct((rows, share), jnp.bfloat16),
+        in_specs=[pl.BlockSpec(memory_space=pl.ANY)] + [pl.BlockSpec(memory_space=pltpu.VMEM)] * 3,
+        out_specs=pl.BlockSpec(memory_space=pltpu.VMEM),
+        scratch_shapes=[
+            pltpu.VMEM((groups, depth, 3 * share), jnp.bfloat16),
+            pltpu.VMEM((rows, width), jnp.bfloat16),
+            pltpu.VMEM((rows, 3 * share), jnp.float32),
+            pltpu.SemaphoreType.DMA((3,)),
+            pltpu.SemaphoreType.DMA((groups, 3)),
+            pltpu.SemaphoreType.DMA((groups, 3)),
+            pltpu.SemaphoreType.DMA((groups,)),
+            pltpu.SemaphoreType.DMA((groups,)),
+        ],
+        compiler_params=pltpu.CompilerParams(
+            collective_id=0, has_side_effects=True, vmem_limit_bytes=44 * 1024 * 1024
+        ),
+        name="attend",
+    )(qkv_local, modulated, q_gain, k_gain)
+
+
+def project_kernel(
+    sections,
+    seqs,
+    batches,
+    att_ref,
+    w_ref,
+    source_ref,
+    gate_ref,
+    samples_ref,
+    out_ref,
+    grad_ref,
+    abuf,
+    acc,
+    psend,
+    precv,
+    cols,
+    gaps,
+    a_send,
+    a_recv,
+    p_send,
+    p_recv,
+    c_send,
+    c_recv,
+    g_send,
+    g_recv,
+):
+    section, seq, batch = (lax.axis_index(name) for name in ("section", "seq", "batch"))
+    me = seq * batches + batch
+    rows, width = source_ref.shape
+    share = w_ref.shape[1]
+    depth = att_ref.shape[1]
+    length = rows * seqs
+    part = width // sections
+    peers = group_peers(seqs, batches)
+    across = []
+    for far in range(sections):
+        for side in range(seqs):
+            to = (lax.rem(section + far, sections), lax.rem(seq + side, seqs))
+            back = (lax.rem(section - far + sections, sections), lax.rem(seq - side + seqs, seqs))
+            across.append(((to[0], to[1], batch), to, back, far, side))
+    greet([p[0] for p in peers[1:]] + [p[0] for p in across if p[3] > 0])
+
+    copies = []
+    for at, (coords, _, _) in enumerate(peers):
+        if at > 0:
+            copy = pltpu.make_async_remote_copy(
+                att_ref, abuf.at[me], a_send.at[at], a_recv.at[at], device_id=coords, device_id_type=MESH
+            )
+            copy.start()
+            copies.append(copy)
+    for at, (_, _, (from_seq, from_batch)) in enumerate(peers):
+        rank = from_seq * batches + from_batch
+        deep = pl.ds(pl.multiple_of(rank * depth, 128), depth)
+        if at > 0:
+            copies[at - 1].wait()
+
+        @pl.loop(0, batches)
+        def _(sample):
+            these = pl.ds(pl.multiple_of(sample * length, length), length)
+            block = att_ref[these, :] if at == 0 else abuf[rank, these, :]
+            term = jnp.dot(block, w_ref[deep, :], preferred_element_type=jnp.float32)
+            if at == 0:
+                acc[these, :] = term
+            else:
+                acc[these, :] += term
+
+    psend[...] = acc[...].astype(jnp.bfloat16)
+    copies = []
+    for at, (coords, (to_seq, to_batch), _) in enumerate(peers):
+        theirs = pl.ds(pl.multiple_of((to_batch * seqs + to_seq) * rows, rows), rows)
+        if at > 0:
+            copy = pltpu.make_async_remote_copy(
+                psend.at[theirs, :], precv.at[me], p_send.at[at], p_recv.at[at], device_id=coords, device_id_type=MESH
+            )
+            copy.start()
+            copies.append(copy)
+    my_rows = pl.ds(pl.multiple_of((batch * seqs + seq) * rows, rows), rows)
+    for at, (_, _, (from_seq, from_batch)) in enumerate(peers):
+        rank = from_seq * batches + from_batch
+        here = pl.ds(pl.multiple_of(rank * share, 128), share)
+        if at > 0:
+            copies[at - 1].wait()
+            proj = precv[rank].astype(jnp.float32)
+        else:
+            proj = acc[my_rows, :]
+        out_ref[:, here] = (source_ref[:, here].astype(jnp.float32) + gate_ref[:, here] * proj).astype(jnp.bfloat16)
+
+    gap = jnp.abs(samples_ref[...].astype(jnp.float32) - out_ref[...].astype(jnp.float32))
+    mine = jnp.sum(gap)
+    gaps[section, seq] = jnp.full(gaps.shape[2:], mine, jnp.float32)
+    copies = []
+    for at, (coords, to, back, far, side) in enumerate(across):
+        if far > 0 and side == 0:
+            theirs = pl.ds(pl.multiple_of(to[0] * part, 128), part)
+            copy = pltpu.make_async_remote_copy(
+                out_ref.at[:, theirs],
+                cols.at[section],
+                c_send.at[far],
+                c_recv.at[far],
+                device_id=coords,
+                device_id_type=MESH,
+            )
+            copy.start()
+            copies.append(copy)
+        if at > 0:
+            copy = pltpu.make_async_remote_copy(
+                gaps.at[section, seq],
+                gaps.at[section, seq],
+                g_send.at[at],
+                g_recv.at[at],
+                device_id=coords,
+                device_id_type=MESH,
+            )
+            copy.start()
+            copies.append(copy)
+    cols[section] = out_ref[:, pl.ds(pl.multiple_of(section * part, 128), part)]
+    for copy in copies:
+        copy.wait()
+    total = gaps[2, 0][:1, :1]
+    for side in range(1, seqs):
+        total = total + gaps[2, side][:1, :1]
+    spread = total / (length * width) + mean_eps
+    real = cols[2].astype(jnp.float32)
+    fake = cols[3].astype(jnp.float32)
+    grad_ref[...] = ((fake - real) / spread).astype(jnp.bfloat16)
+
+
+def project(sections, seqs, batches, attended, out_local, source, gate, samples):
+    groups = seqs * batches
+    rows, width = source.shape
+    share = out_local.shape[1]
+    depth = attended.shape[1]
+    part = width // sections
+    return pl.pallas_call(
+        functools.partial(project_kernel, sections, seqs, batches),
+        out_shape=(
+            jax.ShapeDtypeStruct((rows, width), jnp.bfloat16),
+            jax.ShapeDtypeStruct((rows, part), jnp.bfloat16),
+        ),
+        in_specs=[pl.BlockSpec(memory_space=pltpu.VMEM)] * 5,
+        out_specs=(pl.BlockSpec(memory_space=pltpu.VMEM),) * 2,
+        scratch_shapes=[
+            pltpu.VMEM((groups, rows * groups, depth), jnp.bfloat16),
+            pltpu.VMEM((rows * groups, share), jnp.float32),
+            pltpu.VMEM((rows * groups, share), jnp.bfloat16),
+            pltpu.VMEM((groups, rows, share), jnp.bfloat16),
+            pltpu.VMEM((sections, rows, part), jnp.bfloat16),
+            pltpu.VMEM((sections, seqs, 8, 128), jnp.float32),
+            pltpu.SemaphoreType.DMA((groups,)),
+            pltpu.SemaphoreType.DMA((groups,)),
+            pltpu.SemaphoreType.DMA((groups,)),
+            pltpu.SemaphoreType.DMA((groups,)),
+            pltpu.SemaphoreType.DMA((sections,)),
+            pltpu.SemaphoreType.DMA((sections,)),
+            pltpu.SemaphoreType.DMA((sections * seqs,)),
+            pltpu.SemaphoreType.DMA((sections * seqs,)),
+        ],
+        compiler_params=pltpu.CompilerParams(
+            collective_id=1, has_side_effects=True, vmem_limit_bytes=44 * 1024 * 1024
+        ),
+        name="project",
+    )(attended, out_local, source, gate, samples)
+
+
+def pick_modulate(source, table, level):
+    picked = lax.dynamic_index_in_dim(table, level, 0, keepdims=False)
+    data = source.astype(jnp.float32)
+    center = data - jnp.mean(data, axis=-1, keepdims=True)
+    spread = jnp.mean(center * center, axis=-1, keepdims=True)
+    normed = center * lax.rsqrt(spread + norm_eps)
+    return ((normed * (1.0 + picked[1]) + picked[0]).astype(jnp.bfloat16), picked[2])
+
+
+def by_heads(
+    latent,
+    carried,
+    samples,
+    noise,
+    gen_level,
+    score_level,
+    mod_table,
+    qkv_weight,
+    out_weight,
+    query_gain,
+    key_gain,
+):
+    section = lax.axis_index("section")
+    sections, seqs, batches = (lax.axis_size(name) for name in ("section", "seq", "batch"))
+    sigma = (score_level[0].astype(jnp.float32) + 1.0) / LEVELS
+    noised = (
+        (1.0 - sigma) * samples[0].astype(jnp.float32) + sigma * noise[0].astype(jnp.float32)
+    ).astype(jnp.bfloat16)
+    source = jnp.where(section == 0, latent[0], jnp.where(section == 1, carried[0], noised))
+    level = jnp.where(section >= 2, score_level[0], gen_level[0])
+    modulated, gate = pick_modulate(source, mod_table[0], level)
+    attended = attend(seqs, batches, qkv_weight[0], modulated, query_gain, key_gain)
+    result, own_cols = project(
+        sections, seqs, batches, attended, out_weight[0], source, gate[None], samples[0]
+    )
+    return (result[None, None], own_cols[None])
+
+
 def solution(mesh):
+    groups = mesh.shape["seq"] * mesh.shape["batch"]
+    on_device = by_heads if HEADS % groups == 0 else by_batch
     return jax.shard_map(
         on_device,
         mesh=mesh,

time: 738 us -> 485 us (0.66)
  waiting for transfers between devices: 554 us -> 0 us
  Pallas kernels: 0 us -> 470 us
  local copies, waits for them, and re-layouts: 60.7 us -> 4.58 us
  matrix products: 36.7 us -> 0 us
  blocking collectives: 32.8 us -> 0 us
  starting transfers between devices: 15.6 us -> 0 us
  other arithmetic: 19.3 us -> 4.32 us
  between operations: 16 us -> 2.04 us
    pallas_call x0 -> x2, Pallas kernels: none -> 470 us  [the longest x1 266 us: attend(): pl.pallas_call(functools.partial(attend_kernel, seqs, batches), out_shape...]
    all_to_all x3 -> x0, waiting for transfers between devices: 235 us -> none  [the longest x1 197 us: on_device(): lax.all_to_all(qkv_local.reshape(local_rows, 3, HEADS, HD), 'batch', spli...]
    all_gather x3 -> x0, waiting for transfers between devices: 165 us -> none  [the longest x1 165 us: on_device(): lax.all_gather(mine, 'seq', axis=0, tiled=True)]
    reduce_scatter x1 -> x0, waiting for transfers between devices: 111 us -> none  [on_device(): lax.psum_scatter(jnp.dot(attended, out_rows, preferred_element_type=jnp.f...]
    psum x1 -> x0, waiting for transfers between devices: 43.6 us -> none  [from_root(): return lax.psum(kept, axis)]
    dot_general x27 -> x0, matrix products: 36.7 us -> none  [the longest x12 13.1 us: one_block(): jnp.dot(weight.astype(jnp.bfloat16), v_head, preferred_element_type=jnp.f...]
    all_to_all x1 -> x0, blocking collectives: 27.2 us -> none  [head_attention(): back = lax.all_to_all(mixed, 'seq', split_axis=1, concat_axis=0, tiled=True)]
    all_to_all x4 -> x0, local copies, waits for them, and re-layouts: 16.7 us -> none  [the longest x1 12.1 us: on_device(): lax.all_to_all(qkv_local.reshape(local_rows, 3, HEADS, HD), 'batch', spli...]
  transfers between devices with their start and end apart: 8 -> 0, of which waited for: 6 -> 0; matrix products, arithmetic and copies ran while one was open for 11% -> 0% of each run, Pallas kernels for 0% -> 0%
where the time goes in v1:
time: 485 us; the launch traced here: 480 us
  Pallas kernels  470 us (97%)
    pallas_call x1, Pallas kernels, attend(): pl.pallas_call(functools.partial(attend_kernel, seqs, batches), out_shape...  266 us
    pallas_call x1, Pallas kernels, project(): pl.pallas_call(functools.partial(project_kernel, sections, seqs, batches)...  204 us

profile of v1, /device:TPU:0, one launch (start us, length us, event | category | flops | bytes accessed | tf_op | source)
XLA Modules:
  0.0 480.4 jit_solution(16300450258493539382)
XLA Ops:
  1.9 1.0 dynamic-slice_bitcast_fusion
  3.0 2.5 convert_reduce_fusion
  5.5 0.0 copy-start.3
  5.5 0.0 copy-start.4
  5.5 0.4 fusion.2
  5.9 0.4 fusion.5.mod_ref
  6.3 0.0 copy-done.3
  6.3 0.0 copy-done.4
  6.3 0.0 copy-start
  6.3 3.0 copy-done
  9.3 0.0 copy-start.1
  9.3 0.0 copy-start.2
  9.3 265.6 %attend.1.att_ref = bf16[1024,384]{1,0:T(8,128)(2,1)S(1)} custom-call(bf16[384,9216]{1,0:T(8,128)(2,1)S(1)} %bitcast.31, bf16[128,3072]{1,0:T(8,128)(2,1)S(1)} %fusion.5.mod_ref, f32[1,128]{1,0:T(1,128)S(1)} %copy-done.3, f32[1,128]{1,0:T(1,128)S(1)} %copy-done.4), custom_call_target="tpu_custom_call" | custom-call | tf_op jit(solution)/shard_map/attend/pallas_call | solution.py:262
  274.9 0.0 copy-done.1
  274.9 0.0 copy-done.2
  274.9 203.9 %project.1 = (bf16[128,3072]{1,0:T(8,128)(2,1)S(1)}, bf16[128,768]{1,0:T(8,128)(2,1)S(1)}) custom-call(bf16[1024,384]{1,0:T(8,128)(2,1)S(1)} %attend.1.att_ref, bf16[3072,384]{1,0:T(8,128)(2,1)S(1)} %bitcast.33, bf16[128,3072]{1,0:T(8,128)(2,1)S(1)} %get-tuple-element.7.source_ref, f32[1,3072]{1,0:T(1,128)S(1)} %get-tuple-element.8.gate_ref, ...), custom_call_target="tpu_custom_call" | custom-call | tf_op jit(solution)/shard_map/project/pallas_call | solution.py:417
  478.9 0.9 copy.17
  479.8 0.7 copy.18
  (2 shorter events, 0.0 us)
Async XLA Ops:
  5.5 0.8 copy-start.3
  5.5 0.8 copy-start.4
  6.3 3.0 copy-start
  9.3 265.6 %copy-start.1 = (bf16[1,128,3072]{2,1,0:T(8,128)(2,1)S(1)}, bf16[1,128,3072]{2,1,0:T(8,128)(2,1)}, u32[]{:S(2)}) copy-start(bf16[1,128,3072]{2,1,0:T(8,128)(2,1)} %param.13) | copy-start | bytes 2359300
  9.3 265.6 %copy-start.2 = (bf16[1,3072,384]{2,1,0:T(8,128)(2,1)S(1)}, bf16[1,3072,384]{2,1,0:T(8,128)(2,1)}, u32[]{:S(2)}) copy-start(bf16[1,3072,384]{2,1,0:T(8,128)(2,1)} %param.19) | copy-start | bytes 7077892

commit v2 on v1

--- a/solution.py
+++ b/solution.py
@@ -170,6 +170,119 @@
     return found
 
 
+def gather_slots(seqs, batches):
+    return 2 * batches * (1 + 2 * seqs) + 2 * seqs
+
+
+def gather(seqs, batches, own, place, cut, send_sem, recv_sem, between=lambda step: None):
+    section, seq, batch = (lax.axis_index(name) for name in ("section", "seq", "batch"))
+    rows = own.shape[0]
+    slots = {}
+    sent = []
+
+    def remote(source, target, key, to_seq, to_batch):
+        slot = slots.setdefault(key, len(slots))
+        return pltpu.make_async_remote_copy(
+            source,
+            target,
+            send_sem.at[slot],
+            recv_sem.at[slot],
+            device_id=(section, to_seq, to_batch),
+            device_id_type=MESH,
+        )
+
+    def send(ok, make):
+        if ok is None:
+            make().start()
+        else:
+            pl.when(ok)(lambda: make().start())
+        sent.append((ok, make))
+
+    def bounds(stream):
+        return (0, cut) if stream == 0 else (cut, rows)
+
+    def owner(stream):
+        return seq if stream <= 1 else lax.rem(seq - (stream - 1) + seqs, seqs)
+
+    def push(stream, right, step):
+        if step >= batches:
+            return
+        index = batch - (step - 1) if right else batch + (step - 1)
+        ok = (index >= 0) & (batch + 1 < batches) if right else (index < batches) & (batch >= 1)
+        low, high = bounds(stream)
+
+        def make():
+            target = place(owner(stream), index, low, high)
+            source = own.at[low:high] if step == 1 and stream <= 1 else target
+            return remote(source, target, (stream, right, step), seq, batch + 1 if right else batch - 1)
+
+        send(ok, make)
+
+    def arrived(stream, right, step):
+        index = batch - step if right else batch + step
+        ok = index >= 0 if right else index < batches
+        target = place(owner(stream), index, *bounds(stream))
+        pl.when(ok)(lambda: remote(target, target, (stream, right, step), seq, batch).wait_recv())
+
+    def over(right, step):
+        index = batch - step if right else batch + step
+        ok = None if step == 0 else (index >= 0 if right else index < batches)
+        for side in range(1, seqs):
+
+            def make(side=side):
+                target = place(seq, index, 0, cut)
+                source = own.at[0:cut] if step == 0 else target
+                return remote(source, target, ("over", side, right, step), lax.rem(seq + side, seqs), batch)
+
+            send(ok, make)
+
+    def came_over(right, step):
+        index = batch - step if right else batch + step
+        for side in range(1, seqs):
+            target = place(lax.rem(seq - side + seqs, seqs), index, 0, cut)
+            copy = remote(target, target, ("over", side, right, step), seq, batch)
+            if step == 0:
+                copy.wait_recv()
+            else:
+                pl.when(index >= 0 if right else index < batches)(copy.wait_recv)
+
+    late = list(range(1, seqs + 1)) if cut < rows else []
+    if late:
+        for side in range(1, seqs):
+
+            def make(side=side):
+                target = place(seq, batch, cut, rows)
+                return remote(own.at[cut:rows], target, ("first", side), lax.rem(seq + side, seqs), batch)
+
+            send(None, make)
+    for stream in [0] + late[:1]:
+        for right in (True, False):
+            push(stream, right, 1)
+    over(True, 0)
+    for side in late[1:]:
+        target = place(owner(side), batch, cut, rows)
+        remote(target, target, ("first", side - 1), seq, batch).wait_recv()
+        for right in (True, False):
+            push(side, right, 1)
+    for step in range(1, batches):
+        between(step)
+        for stream in [0] + late:
+            for right in (True, False):
+                arrived(stream, right, step)
+                push(stream, right, step + 1)
+                if stream == 0:
+                    over(right, step)
+    came_over(True, 0)
+    for step in range(1, batches):
+        for right in (True, False):
+            came_over(right, step)
+    for ok, make in sent:
+        if ok is None:
+            make().wait_send()
+        else:
+            pl.when(ok)(lambda make=make: make().wait_send())
+
+
 def attend_kernel(
     seqs, batches, w_ref, mod_ref, qg_ref, kg_ref, out_ref, wbuf, mbuf, acc, own_sem, w_send, w_recv, m_send, m_recv
 ):
@@ -188,40 +301,42 @@
         return pl.ds(pl.multiple_of(part * width + rank * share, 128), share)
 
     my_rows = pl.ds(pl.multiple_of((batch * seqs + seq) * rows, rows), rows)
-    copies = []
-    for at, (coords, _, _) in enumerate(peers):
-        if at == 0:
-            continue
-        copy = pltpu.make_async_remote_copy(
-            mod_ref, mbuf.at[my_rows, :], m_send.at[at], m_recv.at[at], device_id=coords, device_id_type=MESH
-        )
-        copy.start()
-        copies.append(copy)
-    weights = []
-    for at, (coords, (to_seq, to_batch), _) in enumerate(peers):
-        rank = to_seq * batches + to_batch
-        for part in range(3):
-            source = w_ref.at[:, columns(rank, part)]
-            target = wbuf.at[me, :, pl.ds(part * share, share)]
-            if at == 0:
-                copy = pltpu.make_async_copy(source, target, own_sem.at[part])
-            else:
-                copy = pltpu.make_async_remote_copy(
-                    source,
-                    target,
-                    w_send.at[at, part],
-                    w_recv.at[at, part],
-                    device_id=coords,
-                    device_id_type=MESH,
-                )
-            copy.start()
-            weights.append(copy)
     mbuf[my_rows, :] = mod_ref[...]
-    for copy in copies:
-        copy.wait()
+    weights = {}
+
+    def launch(ats):
+        for at in ats:
+            coords, (to_seq, to_batch), _ = peers[at]
+            rank = to_seq * batches + to_batch
+            for part in range(3):
+                source = w_ref.at[:, columns(rank, part)]
+                target = wbuf.at[me, :, pl.ds(part * share, share)]
+                if at == 0:
+                    copy = pltpu.make_async_copy(source, target, own_sem.at[part])
+                else:
+                    copy = pltpu.make_async_remote_copy(
+                        source,
+                        target,
+                        w_send.at[at, part],
+                        w_recv.at[at, part],
+                        device_id=coords,
+                        device_id_type=MESH,
+                    )
+                copy.start()
+                weights[at, part] = copy
+
+    def place(from_seq, from_batch, low, high):
+        first = pl.multiple_of((from_batch * seqs + from_seq) * rows + low, 16)
+        return mbuf.at[pl.ds(first, high - low), :]
+
+    def between(step):
+        if step == 1:
+            launch(list(range(len(peers)))[::-1])
+
+    gather(seqs, batches, mod_ref, place, rows, m_send, m_recv, between)
     for at, (_, _, (from_seq, from_batch)) in enumerate(peers):
         for part in range(3):
-            weights[3 * at + part].wait()
+            weights[at, part].wait()
         rank = from_seq * batches + from_batch
         deep = pl.ds(pl.multiple_of(rank * depth, 128), depth)
 
@@ -271,8 +386,8 @@
             pltpu.SemaphoreType.DMA((3,)),
             pltpu.SemaphoreType.DMA((groups, 3)),
             pltpu.SemaphoreType.DMA((groups, 3)),
-            pltpu.SemaphoreType.DMA((groups,)),
-            pltpu.SemaphoreType.DMA((groups,)),
+            pltpu.SemaphoreType.DMA((gather_slots(seqs, batches),)),
+            pltpu.SemaphoreType.DMA((gather_slots(seqs, batches),)),
         ],
         compiler_params=pltpu.CompilerParams(
             collective_id=0, has_side_effects=True, vmem_limit_bytes=44 * 1024 * 1024
@@ -323,19 +438,13 @@
             across.append(((to[0], to[1], batch), to, back, far, side))
     greet([p[0] for p in peers[1:]] + [p[0] for p in across if p[3] > 0])
 
-    copies = []
-    for at, (coords, _, _) in enumerate(peers):
-        if at > 0:
-            copy = pltpu.make_async_remote_copy(
-                att_ref, abuf.at[me], a_send.at[at], a_recv.at[at], device_id=coords, device_id_type=MESH
-            )
-            copy.start()
-            copies.append(copy)
+    def place(from_seq, from_batch, low, high):
+        return abuf.at[from_seq * batches + from_batch, low:high, :]
+
+    gather(seqs, batches, att_ref, place, att_ref.shape[0] // 2, a_send, a_recv)
     for at, (_, _, (from_seq, from_batch)) in enumerate(peers):
         rank = from_seq * batches + from_batch
         deep = pl.ds(pl.multiple_of(rank * depth, 128), depth)
-        if at > 0:
-            copies[at - 1].wait()
 
         @pl.loop(0, batches)
         def _(sample):
@@ -429,8 +538,8 @@
             pltpu.VMEM((groups, rows, share), jnp.bfloat16),
             pltpu.VMEM((sections, rows, part), jnp.bfloat16),
             pltpu.VMEM((sections, seqs, 8, 128), jnp.float32),
-            pltpu.SemaphoreType.DMA((groups,)),
-            pltpu.SemaphoreType.DMA((groups,)),
+            pltpu.SemaphoreType.DMA((gather_slots(seqs, batches),)),
+            pltpu.SemaphoreType.DMA((gather_slots(seqs, batches),)),
             pltpu.SemaphoreType.DMA((groups,)),
             pltpu.SemaphoreType.DMA((groups,)),
             pltpu.SemaphoreType.DMA((sections,)),

time: 485 us -> 367 us (0.76)
  Pallas kernels: 470 us -> 353 us
    pallas_call x1, Pallas kernels: 204 us -> 107 us  [project(): pl.pallas_call(functools.partial(project_kernel, sections, seqs, batches)...]
    pallas_call x1, Pallas kernels: 266 us -> 246 us  [attend(): pl.pallas_call(functools.partial(attend_kernel, seqs, batches), out_shape...]
where the time goes in v2:
time: 367 us; the launch traced here: 364 us
  Pallas kernels  353 us (96%)
  local copies, waits for them, and re-layouts  4.58 us (1%)
  other arithmetic  4.32 us (1%)
    pallas_call x1, Pallas kernels, attend(): pl.pallas_call(functools.partial(attend_kernel, seqs, batches), out_shape...  246 us
    pallas_call x1, Pallas kernels, project(): pl.pallas_call(functools.partial(project_kernel, sections, seqs, batches)...  107 us

profile of v2, /device:TPU:0, one launch (start us, length us, event | category | flops | bytes accessed | tf_op | source)
XLA Modules:
  0.0 363.9 jit_solution(37510246009119446)
XLA Ops:
  1.9 1.0 dynamic-slice_bitcast_fusion
  3.0 2.5 convert_reduce_fusion
  5.5 0.0 copy-start.3
  5.5 0.0 copy-start.4
  5.5 0.4 fusion.2
  5.9 0.4 fusion.5.mod_ref
  6.3 0.0 copy-done.3
  6.3 0.0 copy-done.4
  6.3 0.0 copy-start
  6.3 3.0 copy-done
  9.3 0.0 copy-start.1
  9.3 0.0 copy-start.2
  9.3 246.4 %attend.1.att_ref = bf16[1024,384]{1,0:T(8,128)(2,1)S(1)} custom-call(bf16[384,9216]{1,0:T(8,128)(2,1)S(1)} %bitcast.31, bf16[128,3072]{1,0:T(8,128)(2,1)S(1)} %fusion.5.mod_ref, f32[1,128]{1,0:T(1,128)S(1)} %copy-done.3, f32[1,128]{1,0:T(1,128)S(1)} %copy-done.4), custom_call_target="tpu_custom_call" | custom-call | tf_op jit(solution)/shard_map/attend/pallas_call | solution.py:377
  255.8 0.0 copy-done.1
  255.8 0.0 copy-done.2
  255.8 106.5 %project.1 = (bf16[128,3072]{1,0:T(8,128)(2,1)S(1)}, bf16[128,768]{1,0:T(8,128)(2,1)S(1)}) custom-call(bf16[1024,384]{1,0:T(8,128)(2,1)S(1)} %attend.1.att_ref, bf16[3072,384]{1,0:T(8,128)(2,1)S(1)} %bitcast.33, bf16[128,3072]{1,0:T(8,128)(2,1)S(1)} %get-tuple-element.7.source_ref, f32[1,3072]{1,0:T(1,128)S(1)} %get-tuple-element.8.gate_ref, ...), custom_call_target="tpu_custom_call" | custom-call | tf_op jit(solution)/shard_map/project/pallas_call | solution.py:526
  362.3 0.9 copy.17
  363.2 0.7 copy.18
  (2 shorter events, 0.0 us)
Async XLA Ops:
  5.5 0.8 copy-start.3
  5.5 0.8 copy-start.4
  6.3 3.0 copy-start
  9.3 246.4 %copy-start.1 = (bf16[1,128,3072]{2,1,0:T(8,128)(2,1)S(1)}, bf16[1,128,3072]{2,1,0:T(8,128)(2,1)}, u32[]{:S(2)}) copy-start(bf16[1,128,3072]{2,1,0:T(8,128)(2,1)} %param.13) | copy-start | bytes 2359300
  9.3 246.4 %copy-start.2 = (bf16[1,3072,384]{2,1,0:T(8,128)(2,1)S(1)}, bf16[1,3072,384]{2,1,0:T(8,128)(2,1)}, u32[]{:S(2)}) copy-start(bf16[1,3072,384]{2,1,0:T(8,128)(2,1)} %param.19) | copy-start | bytes 7077892

commit v3 on v2

--- a/solution.py
+++ b/solution.py
@@ -284,7 +284,7 @@
 
 
 def attend_kernel(
-    seqs, batches, w_ref, mod_ref, qg_ref, kg_ref, out_ref, wbuf, mbuf, acc, own_sem, w_send, w_recv, m_send, m_recv
+    seqs, batches, w_ref, mod_ref, qg_ref, kg_ref, out_ref, wbuf, mbuf, own_sem, w_send, w_recv, m_send, m_recv
 ):
     seq, batch = lax.axis_index("seq"), lax.axis_index("batch")
     groups = seqs * batches
@@ -297,68 +297,60 @@
     peers = group_peers(seqs, batches)
     greet([coords for coords, _, _ in peers[1:]])
 
-    def columns(rank, part):
-        return pl.ds(pl.multiple_of(part * width + rank * share, 128), share)
+    heads = share // HD
+
+    def columns(rank, part, head):
+        return pl.ds(pl.multiple_of(part * width + rank * share + head * HD, 128), HD)
 
     my_rows = pl.ds(pl.multiple_of((batch * seqs + seq) * rows, rows), rows)
     mbuf[my_rows, :] = mod_ref[...]
     weights = {}
 
-    def launch(ats):
-        for at in ats:
+    def launch(head):
+        for at in reversed(range(groups)):
             coords, (to_seq, to_batch), _ = peers[at]
             rank = to_seq * batches + to_batch
             for part in range(3):
-                source = w_ref.at[:, columns(rank, part)]
-                target = wbuf.at[me, :, pl.ds(part * share, share)]
+                slot = 3 * head + part
+                source = w_ref.at[:, columns(rank, part, head)]
+                target = wbuf.at[pl.ds(pl.multiple_of(me * depth, 128), depth), pl.ds(slot * HD, HD)]
                 if at == 0:
-                    copy = pltpu.make_async_copy(source, target, own_sem.at[part])
+                    copy = pltpu.make_async_copy(source, target, own_sem.at[slot])
                 else:
                     copy = pltpu.make_async_remote_copy(
                         source,
                         target,
-                        w_send.at[at, part],
-                        w_recv.at[at, part],
+                        w_send.at[at, slot],
+                        w_recv.at[at, slot],
                         device_id=coords,
                         device_id_type=MESH,
                     )
                 copy.start()
-                weights[at, part] = copy
+                weights[at, slot] = copy
 
     def place(from_seq, from_batch, low, high):
         first = pl.multiple_of((from_batch * seqs + from_seq) * rows + low, 16)
         return mbuf.at[pl.ds(first, high - low), :]
 
     def between(step):
-        if step == 1:
-            launch(list(range(len(peers)))[::-1])
+        for head in range(heads * (step - 1) // (batches - 1), heads * step // (batches - 1)):
+            launch(head)
 
     gather(seqs, batches, mod_ref, place, rows, m_send, m_recv, between)
-    for at, (_, _, (from_seq, from_batch)) in enumerate(peers):
-        for part in range(3):
-            weights[at, part].wait()
-        rank = from_seq * batches + from_batch
-        deep = pl.ds(pl.multiple_of(rank * depth, 128), depth)
+    scale = 1.0 / math.sqrt(HD)
+    for head in range(heads):
+        for at in range(groups):
+            for part in range(3):
+                weights[at, 3 * head + part].wait()
 
         @pl.loop(0, batches)
         def _(sample):
             these = pl.ds(pl.multiple_of(sample * length, length), length)
-            term = jnp.dot(mbuf[these, deep], wbuf[rank], preferred_element_type=jnp.float32)
-            if at == 0:
-                acc[these, :] = term
-            else:
-                acc[these, :] += term
-
-    scale = 1.0 / math.sqrt(HD)
-
-    @pl.loop(0, batches)
-    def _(sample):
-        these = pl.ds(pl.multiple_of(sample * length, length), length)
-        for head in range(share // HD):
-            at = head * HD
-            query = head_norm(acc[these, at : at + HD], qg_ref[...])
-            keys = head_norm(acc[these, share + at : share + at + HD], kg_ref[...])
-            values = acc[these, 2 * share + at : 2 * share + at + HD].astype(jnp.bfloat16)
+            own = wbuf[:, 3 * head * HD : 3 * (head + 1) * HD]
+            qkv = jnp.dot(mbuf[these, :], own, preferred_element_type=jnp.float32)
+            query = head_norm(qkv[:, :HD], qg_ref[...])
+            keys = head_norm(qkv[:, HD : 2 * HD], kg_ref[...])
+            values = qkv[:, 2 * HD :].astype(jnp.bfloat16)
             score = (
                 lax.dot_general(query, keys, (((1,), (1,)), ((), ())), preferred_element_type=jnp.float32) * scale
             )
@@ -366,7 +358,7 @@
             weight = jnp.exp(score - top)
             total = jnp.sum(weight, axis=-1, keepdims=True)
             mixed = jnp.dot(weight.astype(jnp.bfloat16), values, preferred_element_type=jnp.float32)
-            out_ref[these, at : at + HD] = (mixed / total).astype(jnp.bfloat16)
+            out_ref[these, head * HD : (head + 1) * HD] = (mixed / total).astype(jnp.bfloat16)
 
 
 def attend(seqs, batches, qkv_local, modulated, q_gain, k_gain):
@@ -380,12 +372,11 @@
         in_specs=[pl.BlockSpec(memory_space=pl.ANY)] + [pl.BlockSpec(memory_space=pltpu.VMEM)] * 3,
         out_specs=pl.BlockSpec(memory_space=pltpu.VMEM),
         scratch_shapes=[
-            pltpu.VMEM((groups, depth, 3 * share), jnp.bfloat16),
+            pltpu.VMEM((groups * depth, 3 * share), jnp.bfloat16),
             pltpu.VMEM((rows, width), jnp.bfloat16),
-            pltpu.VMEM((rows, 3 * share), jnp.float32),
-            pltpu.SemaphoreType.DMA((3,)),
-            pltpu.SemaphoreType.DMA((groups, 3)),
-            pltpu.SemaphoreType.DMA((groups, 3)),
+            pltpu.SemaphoreType.DMA((3 * share // HD,)),
+            pltpu.SemaphoreType.DMA((groups, 3 * share // HD)),
+            pltpu.SemaphoreType.DMA((groups, 3 * share // HD)),
             pltpu.SemaphoreType.DMA((gather_slots(seqs, batches),)),
             pltpu.SemaphoreType.DMA((gather_slots(seqs, batches),)),
         ],
@@ -408,7 +399,6 @@
     out_ref,
     grad_ref,
     abuf,
-    acc,
     psend,
     precv,
     cols,
@@ -439,42 +429,38 @@
     greet([p[0] for p in peers[1:]] + [p[0] for p in across if p[3] > 0])
 
     def place(from_seq, from_batch, low, high):
-        return abuf.at[from_seq * batches + from_batch, low:high, :]
-
+        first = pl.multiple_of((from_seq * batches + from_batch) * depth, 128)
+        return abuf.at[low:high, pl.ds(first, depth)]
+
+    abuf[:, pl.ds(pl.multiple_of(me * depth, 128), depth)] = att_ref[...]
     gather(seqs, batches, att_ref, place, att_ref.shape[0] // 2, a_send, a_recv)
-    for at, (_, _, (from_seq, from_batch)) in enumerate(peers):
-        rank = from_seq * batches + from_batch
-        deep = pl.ds(pl.multiple_of(rank * depth, 128), depth)
-
-        @pl.loop(0, batches)
-        def _(sample):
-            these = pl.ds(pl.multiple_of(sample * length, length), length)
-            block = att_ref[these, :] if at == 0 else abuf[rank, these, :]
-            term = jnp.dot(block, w_ref[deep, :], preferred_element_type=jnp.float32)
-            if at == 0:
-                acc[these, :] = term
-            else:
-                acc[these, :] += term
-
-    psend[...] = acc[...].astype(jnp.bfloat16)
-    copies = []
-    for at, (coords, (to_seq, to_batch), _) in enumerate(peers):
-        theirs = pl.ds(pl.multiple_of((to_batch * seqs + to_seq) * rows, rows), rows)
-        if at > 0:
-            copy = pltpu.make_async_remote_copy(
-                psend.at[theirs, :], precv.at[me], p_send.at[at], p_recv.at[at], device_id=coords, device_id_type=MESH
-            )
-            copy.start()
-            copies.append(copy)
+    copies = {}
+    for near in reversed(range(batches)):
+        sample = lax.rem(batch + near, batches)
+        these = pl.ds(pl.multiple_of(sample * length, length), length)
+        psend[these, :] = jnp.dot(abuf[these, :], w_ref[...], preferred_element_type=jnp.float32).astype(jnp.bfloat16)
+        for at in range(near * seqs, (near + 1) * seqs):
+            coords, (to_seq, to_batch), _ = peers[at]
+            theirs = pl.ds(pl.multiple_of((to_batch * seqs + to_seq) * rows, rows), rows)
+            if at > 0:
+                copies[at] = pltpu.make_async_remote_copy(
+                    psend.at[theirs, :],
+                    precv.at[me],
+                    p_send.at[at],
+                    p_recv.at[at],
+                    device_id=coords,
+                    device_id_type=MESH,
+                )
+                copies[at].start()
     my_rows = pl.ds(pl.multiple_of((batch * seqs + seq) * rows, rows), rows)
     for at, (_, _, (from_seq, from_batch)) in enumerate(peers):
         rank = from_seq * batches + from_batch
         here = pl.ds(pl.multiple_of(rank * share, 128), share)
         if at > 0:
-            copies[at - 1].wait()
+            copies[at].wait()
             proj = precv[rank].astype(jnp.float32)
         else:
-            proj = acc[my_rows, :]
+            proj = psend[my_rows, :].astype(jnp.float32)
         out_ref[:, here] = (source_ref[:, here].astype(jnp.float32) + gate_ref[:, here] * proj).astype(jnp.bfloat16)
 
     gap = jnp.abs(samples_ref[...].astype(jnp.float32) - out_ref[...].astype(jnp.float32))
@@ -532,8 +518,7 @@
         in_specs=[pl.BlockSpec(memory_space=pltpu.VMEM)] * 5,
         out_specs=(pl.BlockSpec(memory_space=pltpu.VMEM),) * 2,
         scratch_shapes=[
-            pltpu.VMEM((groups, rows * groups, depth), jnp.bfloat16),
-            pltpu.VMEM((rows * groups, share), jnp.float32),
+            pltpu.VMEM((rows * groups, width), jnp.bfloat16),
             pltpu.VMEM((rows * groups, share), jnp.bfloat16),
             pltpu.VMEM((groups, rows, share), jnp.bfloat16),
             pltpu.VMEM((sections, rows, part), jnp.bfloat16),

time: 367 us -> 347 us (0.946)
  Pallas kernels: 353 us -> 334 us
    pallas_call x1, Pallas kernels: 246 us -> 219 us  [attend(): pl.pallas_call(functools.partial(attend_kernel, seqs, batches), out_shape...]
    pallas_call x1, Pallas kernels: 107 us -> 115 us  [project(): pl.pallas_call(functools.partial(project_kernel, sections, seqs, batches)...]
where the time goes in v3:
time: 347 us; the launch traced here: 345 us
  Pallas kernels  334 us (96%)
  local copies, waits for them, and re-layouts  4.58 us (1%)
  other arithmetic  4.32 us (1%)
    pallas_call x1, Pallas kernels, attend(): pl.pallas_call(functools.partial(attend_kernel, seqs, batches), out_shape...  219 us
    pallas_call x1, Pallas kernels, project(): pl.pallas_call(functools.partial(project_kernel, sections, seqs, batches)...  115 us

profile of v3, /device:TPU:0, one launch (start us, length us, event | category | flops | bytes accessed | tf_op | source)
XLA Modules:
  0.0 345.1 jit_solution(18282681753242327457)
XLA Ops:
  1.9 1.0 dynamic-slice_bitcast_fusion
  3.0 2.5 convert_reduce_fusion
  5.5 0.0 copy-start.3
  5.5 0.0 copy-start.4
  5.5 0.4 fusion.2
  5.9 0.4 fusion.5.mod_ref
  6.3 0.0 copy-done.3
  6.3 0.0 copy-done.4
  6.3 0.0 copy-start
  6.3 3.0 copy-done
  9.3 0.0 copy-start.1
  9.3 0.0 copy-start.2
  9.3 219.2 %attend.1.att_ref = bf16[1024,384]{1,0:T(8,128)(2,1)S(1)} custom-call(bf16[384,9216]{1,0:T(8,128)(2,1)S(1)} %bitcast.31, bf16[128,3072]{1,0:T(8,128)(2,1)S(1)} %fusion.5.mod_ref, f32[1,128]{1,0:T(1,128)S(1)} %copy-done.3, f32[1,128]{1,0:T(1,128)S(1)} %copy-done.4), custom_call_target="tpu_custom_call" | custom-call | tf_op jit(solution)/shard_map/attend/pallas_call | solution.py:369
  228.6 0.0 copy-done.1
  228.6 0.0 copy-done.2
  228.6 114.9 %project.1 = (bf16[128,3072]{1,0:T(8,128)(2,1)S(1)}, bf16[128,768]{1,0:T(8,128)(2,1)S(1)}) custom-call(bf16[1024,384]{1,0:T(8,128)(2,1)S(1)} %attend.1.att_ref, bf16[3072,384]{1,0:T(8,128)(2,1)S(1)} %bitcast.33, bf16[128,3072]{1,0:T(8,128)(2,1)S(1)} %get-tuple-element.7.source_ref, f32[1,3072]{1,0:T(1,128)S(1)} %get-tuple-element.8.gate_ref, ...), custom_call_target="tpu_custom_call" | custom-call | tf_op jit(solution)/shard_map/project/pallas_call | solution.py:512
  343.5 0.9 copy.17
  344.4 0.7 copy.18
  (2 shorter events, 0.0 us)
Async XLA Ops:
  5.5 0.8 copy-start.3
  5.5 0.8 copy-start.4
  6.3 3.0 copy-start
  9.3 219.2 %copy-start.1 = (bf16[1,128,3072]{2,1,0:T(8,128)(2,1)S(1)}, bf16[1,128,3072]{2,1,0:T(8,128)(2,1)}, u32[]{:S(2)}) copy-start(bf16[1,128,3072]{2,1,0:T(8,128)(2,1)} %param.13) | copy-start | bytes 2359300
  9.3 219.2 %copy-start.2 = (bf16[1,3072,384]{2,1,0:T(8,128)(2,1)S(1)}, bf16[1,3072,384]{2,1,0:T(8,128)(2,1)}, u32[]{:S(2)}) copy-start(bf16[1,3072,384]{2,1,0:T(8,128)(2,1)} %param.19) | copy-start | bytes 7077892

commit v4 on v3

--- a/solution.py
+++ b/solution.py
@@ -336,7 +336,7 @@
         for head in range(heads * (step - 1) // (batches - 1), heads * step // (batches - 1)):
             launch(head)
 
-    gather(seqs, batches, mod_ref, place, rows, m_send, m_recv, between)
+    gather(seqs, batches, mod_ref, place, rows // 2, m_send, m_recv, between)
     scale = 1.0 / math.sqrt(HD)
     for head in range(heads):
         for at in range(groups):

time: 347 us -> 337 us (0.971)
  Pallas kernels: 334 us -> 326 us
    pallas_call x1, Pallas kernels: 115 us -> 108 us  [project(): pl.pallas_call(functools.partial(project_kernel, sections, seqs, batches)...]
where the time goes in v4:
time: 337 us
  Pallas kernels  326 us (97%)
  local copies, waits for them, and re-layouts  4.58 us (1%)
  other arithmetic  4.32 us (1%)
    pallas_call x1, Pallas kernels, attend(): pl.pallas_call(functools.partial(attend_kernel, seqs, batches), out_shape...  217 us
    pallas_call x1, Pallas kernels, project(): pl.pallas_call(functools.partial(project_kernel, sections, seqs, batches)...  108 us

profile of v4, /device:TPU:0, one launch (start us, length us, event | category | flops | bytes accessed | tf_op | source)
XLA Modules:
  0.0 336.9 jit_solution(3904060130671217140)
XLA Ops:
  1.9 1.0 dynamic-slice_bitcast_fusion
  3.0 2.5 convert_reduce_fusion
  5.5 0.0 copy-start.3
  5.5 0.0 copy-start.4
  5.5 0.4 fusion.2
  5.9 0.4 fusion.5.mod_ref
  6.3 0.0 copy-done.3
  6.3 0.0 copy-done.4
  6.3 0.0 copy-start
  6.3 3.0 copy-done
  9.3 0.0 copy-start.1
  9.3 0.0 copy-start.2
  9.3 217.5 %attend.1.att_ref = bf16[1024,384]{1,0:T(8,128)(2,1)S(1)} custom-call(bf16[384,9216]{1,0:T(8,128)(2,1)S(1)} %bitcast.31, bf16[128,3072]{1,0:T(8,128)(2,1)S(1)} %fusion.5.mod_ref, f32[1,128]{1,0:T(1,128)S(1)} %copy-done.3, f32[1,128]{1,0:T(1,128)S(1)} %copy-done.4), custom_call_target="tpu_custom_call" | custom-call | tf_op jit(solution)/shard_map/attend/pallas_call | solution.py:369
  226.9 0.0 copy-done.1
  226.9 0.0 copy-done.2
  226.9 108.4 %project.1 = (bf16[128,3072]{1,0:T(8,128)(2,1)S(1)}, bf16[128,768]{1,0:T(8,128)(2,1)S(1)}) custom-call(bf16[1024,384]{1,0:T(8,128)(2,1)S(1)} %attend.1.att_ref, bf16[3072,384]{1,0:T(8,128)(2,1)S(1)} %bitcast.33, bf16[128,3072]{1,0:T(8,128)(2,1)S(1)} %get-tuple-element.7.source_ref, f32[1,3072]{1,0:T(1,128)S(1)} %get-tuple-element.8.gate_ref, ...), custom_call_target="tpu_custom_call" | custom-call | tf_op jit(solution)/shard_map/project/pallas_call | solution.py:512
  335.3 0.9 copy.17
  336.2 0.7 copy.18
  (2 shorter events, 0.0 us)
Async XLA Ops:
  5.5 0.8 copy-start.3
  5.5 0.8 copy-start.4
  6.3 3.0 copy-start
  9.3 217.5 %copy-start.1 = (bf16[1,128,3072]{2,1,0:T(8,128)(2,1)S(1)}, bf16[1,128,3072]{2,1,0:T(8,128)(2,1)}, u32[]{:S(2)}) copy-start(bf16[1,128,3072]{2,1,0:T(8,128)(2,1)} %param.13) | copy-start | bytes 2359300
  9.3 217.5 %copy-start.2 = (bf16[1,3072,384]{2,1,0:T(8,128)(2,1)S(1)}, bf16[1,3072,384]{2,1,0:T(8,128)(2,1)}, u32[]{:S(2)}) copy-start(bf16[1,3072,384]{2,1,0:T(8,128)(2,1)} %param.19) | copy-start | bytes 7077892
